TPU v7x, 1024 devices: a whole 4x8x16 slice. The times are simulated.
1024 devices in a mesh: col: 16 (over z), node: 64 (over y, x, core).
Axes of the slice: x: 4, y: 8, z: 16, core: 2. Of those that a mesh axis runs over, the one named last changes fastest.
Arguments:
- features: bfloat16 [65536, 4096], P('node', 'col'), may hold values from -6 to 6
- seed_ids: int32 [16384], P('node'), may hold values from 0 to 1023
- send_rows: int32 [64, 64, 16], P('node'), may hold values from 0 to 1023
- send_counts: int32 [64, 64], P('node'), may hold values from 1 to 16, as said below
- tile_src: int32 [128, 16], P('node'), may hold values from 0 to 15
- tile_weights: bfloat16 [128, 16, 128, 128], P('node'), may hold values from -0.125 to 0.125
- w_self: bfloat16 [4096, 1024], P('col'), may hold values from -0.0625 to 0.0625
- w_neigh: bfloat16 [4096, 1024], P('col'), may hold values from -0.0625 to 0.0625
- cotangent: bfloat16 [16384, 1024], P('node'), may hold values from -0.059814453 to 0.059814453
Outputs:
- hidden: bfloat16 [16384, 1024], P('node', 'col')
- grad_self: float32 [4096, 1024], P(('col', 'node'))
- grad_neigh: float32 [4096, 1024], P(('col', 'node'))
Inputs may be any that keep to these rules, and one draw needn't show every extreme that they name: `send_counts`: live slots from one shard to another; in every draw one receiving shard gets 16 from every sender.
All inputs are finite; a program needn't handle non-finite values.
Results may differ from a plain program's by a relative error of at most 0.0051.
Values may be sent and summed in bfloat16 or wider, within the bound.
A program may use at most 32 MiB of HBM per device.

v0:
```python
import jax
import jax.numpy as jnp
from jax import lax
from jax.sharding import PartitionSpec as P


def silu_slope(pre):
    sig = jax.nn.sigmoid(pre)
    return sig * (1.0 + pre * (1.0 - sig))


def on_device(
    features, seed_ids, send_rows, send_counts, tile_src, tile_weights, w_self, w_neigh, cotangent
):
    peers = send_rows.shape[1]
    slots = send_rows.shape[2]
    columns = features.shape[1]
    picked = features[send_rows[0]]
    slot_ids = lax.broadcasted_iota(jnp.int32, (peers, slots), 1)
    live_slots = slot_ids < send_counts[0][:, None]
    outgoing = jnp.where(live_slots[:, :, None], picked, jnp.zeros_like(picked))
    self_features = features[seed_ids]
    self_part = jnp.dot(self_features, w_self, preferred_element_type=jnp.float32)
    incoming = lax.all_to_all(outgoing, "node", split_axis=0, concat_axis=0, tiled=True)
    sources = jnp.concatenate([features, incoming.reshape(peers * slots, columns)], axis=0).reshape(
        -1, 128, columns
    )
    blocks = sources[tile_src]
    neighbour_sum = jnp.einsum(
        "skij,skjc->sic", tile_weights, blocks, preferred_element_type=jnp.float32
    )
    neighbour_mean = neighbour_sum.reshape(seed_ids.shape[0], columns).astype(jnp.bfloat16)
    partial_value = self_part + jnp.dot(neighbour_mean, w_neigh, preferred_element_type=jnp.float32)
    groups = lax.axis_size("col")
    share_width = cotangent.shape[1] // groups
    full_sum = lax.psum(partial_value, "col")
    hidden_full = jax.nn.silu(full_sum).astype(jnp.bfloat16)
    hidden = lax.dynamic_slice_in_dim(
        hidden_full, lax.axis_index("col") * share_width, share_width, 1
    )
    grad_pre = (cotangent.astype(jnp.float32) * silu_slope(full_sum)).astype(jnp.bfloat16)
    term_self = lax.dot_general(
        self_features, grad_pre, (((0,), (0,)), ((), ())), preferred_element_type=jnp.float32
    )
    term_neigh = lax.dot_general(
        neighbour_mean, grad_pre, (((0,), (0,)), ((), ())), preferred_element_type=jnp.float32
    )
    grad_self, grad_neigh = (
        lax.psum_scatter(term_self, "node", scatter_dimension=0, tiled=True),
        lax.psum_scatter(term_neigh, "node", scatter_dimension=0, tiled=True),
    )
    return (hidden, grad_self, grad_neigh)


def solution(mesh):
    in_specs = (
        P("node", "col"),
        P("node"),
        P("node", None, None),
        P("node", None),
        P("node", None),
        P("node", None, None, None),
        P("col", None),
        P("col", None),
        P("node", None),
    )
    out_specs = (P("node", "col"), P(("col", "node"), None), P(("col", "node"), None))
    return jax.shard_map(
        on_device, mesh=mesh, in_specs=in_specs, out_specs=out_specs, check_vma=False
    )
```

profile of v0, /device:TPU:1, one launch (start us, length us, event | category | flops | bytes accessed | tf_op | source)
XLA Modules:
  0.0 427.5 jit_solution(16022196029794253537)
XLA Ops:
  7.2 0.0 copy-start
  7.2 0.8 compare_select_fusion
  8.0 0.7 iota_compare_fusion
  8.7 0.1 copy.15
  8.8 0.1 reshape.76
  8.9 4.6 %gather_fusion.1 = bf16[1024,256]{1,0:T(8,128)(2,1)S(1)} fusion(bf16[1024,256]{1,0:T(8,128)(2,1)} %param.9, s32[1024]{0:T(1024)S(1)} %broadcast_clamp_fusion), kind=kCustom, calls=%fused_computation.1 | custom fusion | bytes 1052672 | tf_op jit(solution)/shard_map/gather | solution.py:18
  13.5 0.0 copy-start.5
  13.5 0.0 copy-start.6
  13.5 0.0 copy-start.1
  13.5 0.0 copy-start.3
  13.5 1.0 broadcast_select_fusion
  14.5 18.2 %all-to-all-start = ((bf16[64,16,256]{2,1,0:T(8,128)(2,1)}), bf16[64,16,256]{2,1,0:T(8,128)(2,1)S(1)}, u32[]{:S(2)}, u32[]{:S(2)}) async-start(bf16[64,16,256]{2,1,0:T(8,128)(2,1)} %broadcast_select_fusion), calls=%async_computation | async-start | bytes 1048576 | tf_op jit(solution)/shard_map/all_to_all | solution.py:24
  32.7 0.0 all-reduce.6.cloned.1.call-start
  32.8 0.0 copy-done.5
  32.8 0.1 reshape.84
  32.9 0.0 copy-done.6
  32.9 0.0 copy-done.1
  32.9 1.2 gather_fusion
  34.1 0.0 copy-done.3
  34.1 1.3 fusion.2
  35.4 15.2 %all-to-all-done = bf16[64,16,256]{2,1,0:T(8,128)(2,1)S(1)} async-done(((bf16[64,16,256]{2,1,0:T(8,128)(2,1)}), bf16[64,16,256]{2,1,0:T(8,128)(2,1)S(1)}, u32[]{:S(2)}, u32[]{:S(2)}) %all-to-all-start) | async-done | bytes 524320 | tf_op jit(solution)/shard_map/all_to_all | solution.py:24
  50.6 0.1 pad_maximum_fusion
  50.6 2.0 gather_fusion.2
  52.6 0.0 copy-start.2
  52.6 0.0 copy-start.4
  52.6 0.0 copy-done
  52.6 2.1 fusion
  54.8 0.0 copy-done.2
  54.8 0.0 copy-done.4
  54.8 1.3 convolution_add_fusion
  56.1 0.0 all-reduce.6.cloned.1.call-update
  56.2 0.0 all-reduce.8.cloned.1.call-start
  56.2 132.2 %all-reduce.6.cloned.1.call-done = f32[256,1024]{1,0:T(8,128)} async-done(((f32[256,1024]{1,0:T(8,128)}), f32[256,1024]{1,0:T(8,128)}) %all-reduce.6.cloned.1.call-update) | async-done | bytes 1048592 | tf_op jit(solution)/shard_map/psum | solution.py:36
  188.4 1.8 multiply_convert_fusion
  190.2 1.3 fusion.4
  191.4 1.3 fusion.3
  192.8 0.0 all-reduce.8.cloned.1.call-update
  192.8 1.3 dynamic-slice
  194.7 1.0 fusion.1
  195.8 0.7 copy.16
  196.5 222.8 %all-reduce.8.cloned.1.call-done = (f32[256,1024]{1,0:T(8,128)}, f32[256,1024]{1,0:T(8,128)}) async-done(((f32[256,1024]{1,0:T(8,128)}, f32[256,1024]{1,0:T(8,128)}), (f32[256,1024]{1,0:T(8,128)}, f32[256,1024]{1,0:T(8,128)})) %all-reduce.8.cloned.1.call-update) | async-done | bytes 2097168
  419.3 1.4 constant_dynamic-slice_fusion
  (5 shorter events, 0.0 us)
Async XLA Ops:
  7.2 45.5 %copy-start = (bf16[2,16,128,128]{3,2,1,0:T(8,128)(2,1)S(1)}, bf16[2,16,128,128]{3,2,1,0:T(8,128)(2,1)}, u32[]{:S(2)}) copy-start(bf16[2,16,128,128]{3,2,1,0:T(8,128)(2,1)} %param.14) | copy-start | bytes 3145732
  13.5 19.3 %copy-start.5 = (s32[2,16]{1,0:T(2,128)S(1)}, s32[2,16]{1,0:T(2,128)}, u32[]{:S(2)}) copy-start(s32[2,16]{1,0:T(2,128)} %param.13) | copy-start | bytes 388
  13.5 19.4 %copy-start.6 = (s32[256]{0:T(256)S(1)}, s32[256]{0:T(256)}, u32[]{:S(2)}) copy-start(s32[256]{0:T(256)} %param.10) | copy-start | bytes 3076
  13.5 19.4 %copy-start.1 = (bf16[1024,256]{1,0:T(8,128)(2,1)S(1)}, bf16[1024,256]{1,0:T(8,128)(2,1)}, u32[]{:S(2)}) copy-start(bf16[1024,256]{1,0:T(8,128)(2,1)} %param.9) | copy-start | bytes 1572868
  13.5 20.6 %copy-start.3 = (bf16[256,1024]{1,0:T(8,128)(2,1)S(1)}, bf16[256,1024]{1,0:T(8,128)(2,1)}, u32[]{:S(2)}) copy-start(bf16[256,1024]{1,0:T(8,128)(2,1)} %param.15) | copy-start | bytes 1572868
  14.5 36.1 %all-to-all-start = ((bf16[64,16,256]{2,1,0:T(8,128)(2,1)}), bf16[64,16,256]{2,1,0:T(8,128)(2,1)S(1)}, u32[]{:S(2)}, u32[]{:S(2)}) async-start(bf16[64,16,256]{2,1,0:T(8,128)(2,1)} %broadcast_select_fusion), calls=%async_computation | async-start | bytes 1048576 | tf_op jit(solution)/shard_map/all_to_all | solution.py:24
  32.7 155.6 %all-reduce.6.cloned.1.call-start = ((), (), s32[]{:S(2)}) async-start(), calls=%async_computation.1 | async-start | bytes 2097152 | tf_op jit(solution)/shard_map/psum | solution.py:36
  52.6 2.2 copy-start.2
  52.6 2.2 copy-start.4
  56.2 363.1 %all-reduce.8.cloned.1.call-start = ((), (), s32[]{:S(2)}) async-start(), calls=%async_computation.2 | async-start | bytes 4194304
Sparse Core Ops, SparseCore 0:
  56.3 132.0 all-reduce.5
  192.9 226.3 all-reduce.7
where the time goes:
time: 429 us; the launch traced here: 428 us
  waiting for transfers between devices  370 us (86%)
  starting transfers between devices  18.3 us (4%)
  between operations  14.8 us (3%)
  local copies, waits for them, and re-layouts  11.4 us (3%)
  matrix products  7.34 us (2%)
  other arithmetic  5.44 us (1%)
    unnamed x3, waiting for transfers between devices  223 us
    psum x1, waiting for transfers between devices, on_device(): full_sum = lax.psum(partial_value, 'col')  132 us
    all_to_all x1, starting transfers between devices, on_device(): lax.all_to_all(outgoing, 'node', split_axis=0, concat_axis=0, tiled=True)  18.2 us
    all_to_all x1, waiting for transfers between devices, on_device(): lax.all_to_all(outgoing, 'node', split_axis=0, concat_axis=0, tiled=True)  15.2 us
  transfers between devices with their start and end apart: 3, of which 3 were waited for; matrix products, arithmetic and copies ran while one was open for 1% of the time, Pallas kernels for 0%

commit v1 on v0

v1 whole, which is shorter than its diff:
```python
import jax
import jax.numpy as jnp
from jax import lax
from jax.experimental import pallas as pl
from jax.experimental.pallas import tpu as pltpu
from jax.sharding import PartitionSpec as P

MESH = pl.DeviceIdType.MESH
F32 = jnp.float32
BF16 = jnp.bfloat16

NZ, NY, NX, NC = 16, 8, 4, 2
NN = NY * NX * NC

PARENT = {
    8: 6, 7: 6, 5: 6, -7: -6, -5: -6, 6: 3, -6: -3,
    4: 3, 2: 3, -4: -3, -2: -3, 3: 0, -3: 0, 1: 0, -1: 0,
}
LEAVES = (8, 7, -7, 5, -5, 4, -4, 2, -2, 1, -1)
GROUPS = ((0, 1, -1, 3), (-3, 2, -2, 4), (-4, 6, -6, 5), (7, -5, -7, 8))


def slot(offset):
    return offset % NZ


def left_half(shape):
    return lax.broadcasted_iota(jnp.int32, shape, 1) < 64


def one_hot_rows(row):
    spread = jnp.broadcast_to(row.astype(F32), (128, 128)).T
    lane = lax.broadcasted_iota(jnp.int32, (128, 128), 1).astype(F32)
    parts = [
        jnp.where(spread == lane + 128.0 * j, 1.0, 0.0).astype(BF16) for j in range(8)
    ]
    return jnp.concatenate(parts, axis=1)


def kernel(
    feat, idx, seed, tsrc, tw_hbm, ws_hbm, wn_hbm, cot_hbm,
    hid, gs, gn,
    src, out, tw, ws, wn, cot, sf, nm, part, pk, pkb, rb, sb, cp, ag, xpt, stack,
    cs, cr, xs, xr, ys, yr, fin,
    lsem, a_send, a_recv, b_send, b_recv, c_send, c_recv,
    dc_send, dc_recv, dx_send, dx_recv, dy_send, dy_recv,
):
    z = lax.axis_index("col")
    node = lax.axis_index("node")
    core = node % NC
    x = (node // NC) % NX
    y = node // (NC * NX)

    def zat(offset):
        return (z + offset + NZ) % NZ

    loads = [
        pltpu.make_async_copy(a, b, lsem.at[i])
        for i, (a, b) in enumerate((
            (feat, src.at[pl.ds(0, NN)]), (ws_hbm, ws), (tw_hbm, tw), (wn_hbm, wn), (cot_hbm, cot),
        ))
    ]
    for load in loads:
        load.start()

    barrier = pltpu.get_barrier_semaphore()

    @pl.loop(1, NN)
    def _(k):
        pl.semaphore_signal(
            barrier, inc=1, device_id=(z, (node + k) % NN), device_id_type=MESH
        )

    for d in (1, -1, 2, -2, 3, -3):
        pl.semaphore_signal(barrier, inc=1, device_id=(zat(d), node), device_id_type=MESH)
    loads[0].wait()
    feats = src[pl.ds(0, NN)].reshape(1024, 256)

    def gather(yy):
        hot = one_hot_rows(idx[pl.ds(yy, 1), :])
        rows = jnp.dot(hot, feats, preferred_element_type=F32).astype(BF16)
        out[pl.ds(pl.multiple_of(yy * 8, 8), 8)] = rows.reshape(8, 16, 256)

    def send_rows(to):
        pltpu.make_async_remote_copy(
            src_ref=out.at[to], dst_ref=src.at[NN + node], send_sem=a_send, recv_sem=a_recv,
            device_id=(z, to), device_id_type=MESH,
        ).start()

    for step, d in enumerate((4, 3, 5, 2, 6, 1, 7)):
        yy = (y + d) % NY
        gather(yy)
        if step == 0:
            pl.semaphore_wait(barrier, NN - 1 + 6)
        for j in range(8):
            send_rows(yy * 8 + j)
    gather(y)
    for j in range(1, 8):
        send_rows(y * 8 + (node + j) % 8)
    own = pltpu.make_async_copy(out.at[node], src.at[NN + node], lsem.at[5])
    own.start()

    for b in range(2):
        hot = one_hot_rows(seed[pl.ds(b, 1), :])
        sf[pl.ds(b * 128, 128), :] = jnp.dot(hot, feats, preferred_element_type=F32).astype(BF16)
    loads[1].wait()
    part[...] = jnp.dot(sf[...], ws[...], preferred_element_type=F32)

    r = lax.broadcasted_iota(jnp.int32, (512, 512), 0)
    c = lax.broadcasted_iota(jnp.int32, (512, 512), 1)
    tensor = (r >> 2) & 1
    wanted = (
        tensor * 256 + ((r >> 3) & 7) * 32 + ((r >> 6) & 3) * 8 + (r >> 8) * 4 + (r & 3)
    )
    perm = jnp.where(c == wanted, 1.0, 0.0).astype(BF16)
    stack[...] = perm
    nt = (((1,), (1,)), ((), ()))

    loads[4].wait()
    pair = pl.ds(pl.multiple_of((z // 2) * 128, 128), 128)
    c0 = cot[0:128, pair].astype(F32)
    c1 = cot[128:256, pair].astype(F32)
    even = z % 2 == 0
    left = left_half((128, 128))
    cp[...] = jnp.where(
        left,
        jnp.where(even, c0, pltpu.roll(c0, 64, 1)),
        jnp.where(even, pltpu.roll(c1, 64, 1), c1),
    )
    loads[2].wait()
    loads[3].wait()

    own.wait()
    pltpu.make_async_remote_copy(
        src_ref=src.at[pl.ds(0, NN - 1)], dst_ref=src.at[pl.ds(NN, NN - 1)],
        send_sem=a_send, recv_sem=a_recv, device_id=(z, node), device_id_type=MESH,
    ).wait_recv()
    for b in range(2):
        total = jnp.zeros((128, 256), F32)
        for k in range(0, 16, 2):
            weight = jnp.concatenate([tw[b, k], tw[b, k + 1]], axis=1)
            block = jnp.concatenate(
                [src[pl.ds(tsrc[b, k + e] * 8, 8)].reshape(128, 256) for e in range(2)], axis=0
            )
            total += jnp.dot(weight, block, preferred_element_type=F32)
        nm[pl.ds(b * 128, 128), :] = total.astype(BF16)
    for p in range(8):
        cols = pl.ds(p * 128, 128)
        value = part[:, cols] + jnp.dot(nm[...], wn[:, cols], preferred_element_type=F32)
        p0, p1 = value[0:128], value[128:256]
        first = jnp.where(left, p0, pltpu.roll(p1, 64, 1))
        second = jnp.where(left, pltpu.roll(p0, 64, 1), p1)
        pk[2 * p] = first
        pk[2 * p + 1] = second
        pkb[2 * p] = first.astype(BF16)
        pkb[2 * p + 1] = second.astype(BF16)

    def up(o, source):
        return pltpu.make_async_remote_copy(
            src_ref=source, dst_ref=rb.at[slot(o)],
            send_sem=b_send.at[slot(o)], recv_sem=b_recv.at[slot(o)],
            device_id=(zat(PARENT[o] - o), node), device_id_type=MESH,
        )

    ups = {o: up(o, pkb.at[zat(-o)]) for o in LEAVES}
    for o in LEAVES:
        ups[o].start()

    xpt[...] = (
        lax.dot_general(stack[:, 0:256], sf[...], nt, preferred_element_type=F32)
        + lax.dot_general(stack[:, 256:512], nm[...], nt, preferred_element_type=F32)
    ).astype(BF16)

    def summed(o, children):
        value = pk[zat(-o)]
        for child in children:
            ups[child].wait_recv()
            value = value + rb[slot(child)].astype(F32)
        return value

    for o, children in ((6, (7, 5, 8)), (-6, (-7, -5)), (3, (4, 2, 6)), (-3, (-4, -2, -6))):
        sb[slot(o)] = summed(o, children).astype(BF16)
        ups[o] = up(o, sb.at[slot(o)])
        ups[o].start()
    pre = summed(0, (1, -1, 3, -3))

    s = jax.nn.sigmoid(pre)
    slope = s * (1.0 + pre * (1.0 - s))
    ag[0] = (cp[...] * slope).astype(BF16)

    def down(o):
        return pltpu.make_async_remote_copy(
            src_ref=ag.at[slot(PARENT[o])], dst_ref=ag.at[slot(o)],
            send_sem=c_send.at[slot(o)], recv_sem=c_recv.at[slot(o)],
            device_id=(zat(o - PARENT[o]), node), device_id_type=MESH,
        )

    downs = {}

    def forward(*offsets):
        for o in offsets:
            downs[o] = down(o)
            downs[o].start()

    def arrived(*offsets):
        for o in offsets:
            downs[o].wait_recv()

    forward(3, -3, 1, -1)
    value = pre * s
    hid[0:128, :] = value[:, 0:64].astype(BF16)
    hid[128:256, :] = pltpu.roll(value, 64, 1)[:, 0:64].astype(BF16)

    own_rows = pl.ds(pl.multiple_of(core * 256, 256), 256)
    other_rows = pl.ds(pl.multiple_of((1 - core) * 256, 256), 256)
    kept, copies = {}, {}

    def terms(g):
        halves = []
        for q in (0, 2):
            a = ag[slot(GROUPS[g][q])].astype(F32)
            b = ag[slot(GROUPS[g][q + 1])].astype(F32)
            halves.append(jnp.concatenate(
                [
                    jnp.where(left, a, pltpu.roll(b, 64, 1)),
                    jnp.where(left, pltpu.roll(a, 64, 1), b),
                ], axis=0,
            ).astype(BF16))
        grad = jnp.concatenate(halves, axis=1)
        cs[g] = jnp.dot(xpt[other_rows, :], grad, preferred_element_type=F32).astype(BF16)
        copies["c", g] = pltpu.make_async_remote_copy(
            src_ref=cs.at[g], dst_ref=cr.at[g], send_sem=dc_send.at[g], recv_sem=dc_recv.at[g],
            device_id=(z, node + 1 - 2 * core), device_id_type=MESH,
        )
        copies["c", g].start()
        kept[g] = jnp.dot(xpt[own_rows, :], grad, preferred_element_type=F32)

    def over_x(g):
        copies["c", g].wait_recv()
        total = kept[g] + cr[g].astype(F32)
        for xx in range(4):
            xs[g, xx] = total[xx * 64:(xx + 1) * 64]
        for xx in range(4):
            cs[g, pl.ds(xx * 64, 64)] = total[xx * 64:(xx + 1) * 64].astype(BF16)

    def start_x(g):
        copies["c", g].wait_send()
        over_x(g)
        for i in range(1, NX):
            to = (x + i) % NX
            pltpu.make_async_remote_copy(
                src_ref=cs.at[g, pl.ds(pl.multiple_of(to * 64, 64), 64)], dst_ref=xr.at[g, i - 1],
                send_sem=dx_send.at[g], recv_sem=dx_recv.at[g],
                device_id=(z, (y * NX + to) * NC + core), device_id_type=MESH,
            ).start()

    def all_x(g):
        return pltpu.make_async_remote_copy(
            src_ref=xr.at[g], dst_ref=xr.at[g], send_sem=dx_send.at[g], recv_sem=dx_recv.at[g],
            device_id=(z, node), device_id_type=MESH,
        )

    def all_y(g):
        return pltpu.make_async_remote_copy(
            src_ref=yr.at[g], dst_ref=yr.at[g], send_sem=dy_send.at[g], recv_sem=dy_recv.at[g],
            device_id=(z, node), device_id_type=MESH,
        )

    def start_y(g):
        all_x(g).wait_recv()
        total = xs[g, x]
        for i in range(NX - 1):
            total = total + xr[g, i].astype(F32)
        ys[g] = total.reshape(NY, 8, 256)
        for i in (4, 3, 5, 2, 6, 1, 7):
            to = (y + i) % NY
            pltpu.make_async_remote_copy(
                src_ref=ys.at[g, to], dst_ref=yr.at[g, i - 1],
                send_sem=dy_send.at[g], recv_sem=dy_recv.at[g],
                device_id=(z, (to * NX + x) * NC + core), device_id_type=MESH,
            ).start()

    half = lax.broadcasted_iota(jnp.int32, (8, 128), 1) // 64

    def finish(g):
        all_y(g).wait_recv()
        total = ys[g, y]
        for i in range(NY - 1):
            total = total + yr[g, i]
        for q in range(4):
            chunk = zat(-GROUPS[g][q])
            side = chunk % 2
            tile = total[:, (q // 2) * 128:(q // 2 + 1) * 128]
            tile = jnp.where(side == q % 2, tile, pltpu.roll(tile, 64, 1))
            fin[chunk // 2] = jnp.where(half == side, tile, fin[chunk // 2])

    fin[...] = jnp.zeros_like(fin)
    arrived(3)
    forward(6, 4, 2)
    arrived(-3)
    forward(-6, -4, -2)
    arrived(1, -1)
    terms(0)
    arrived(6)
    forward(8, 7, 5)
    arrived(-6)
    forward(-7, -5)
    arrived(2, -2, 4)
    terms(1)
    start_x(0)
    arrived(-4, 5)
    terms(2)
    start_x(1)
    start_y(0)
    arrived(7, -5, -7, 8)
    terms(3)
    start_x(2)
    start_y(1)
    start_x(3)
    start_y(2)
    finish(0)
    start_y(3)
    finish(1)
    finish(2)
    finish(3)
    for p in range(8):
        cols = pl.ds(p * 128, 128)
        gs[:, cols] = fin[p, 0:4, :]
        gn[:, cols] = fin[p, 4:8, :]

    pltpu.make_async_remote_copy(
        src_ref=out.at[pl.ds(0, NN - 1)], dst_ref=out.at[pl.ds(0, NN - 1)],
        send_sem=a_send, recv_sem=a_recv, device_id=(z, node), device_id_type=MESH,
    ).wait_send()
    for o in PARENT:
        ups[o].wait_send()
        downs[o].wait_send()
    for g in range(4):
        all_x(g).wait_send()
        all_y(g).wait_send()


def on_device(
    features, seed_ids, send_rows, send_counts, tile_src, tile_weights, w_self, w_neigh, cotangent
):
    slot_ids = lax.broadcasted_iota(jnp.int32, send_rows.shape[1:], 1)
    live = slot_ids < send_counts[0][:, None]
    idx = jnp.where(live, send_rows[0], -1).reshape(8, 128)
    any_space = pl.BlockSpec(memory_space=pl.ANY)
    vmem = pl.BlockSpec(memory_space=pltpu.VMEM)
    smem = pl.BlockSpec(memory_space=pltpu.SMEM)
    dma = pltpu.SemaphoreType.DMA
    return pl.pallas_call(
        kernel,
        out_shape=(
            jax.ShapeDtypeStruct((256, 64), BF16),
            jax.ShapeDtypeStruct((4, 1024), F32),
            jax.ShapeDtypeStruct((4, 1024), F32),
        ),
        in_specs=[any_space, vmem, vmem, smem, any_space, any_space, any_space, any_space],
        out_specs=(vmem, vmem, vmem),
        scratch_shapes=[
            pltpu.VMEM((2 * NN, 16, 256), BF16),
            pltpu.VMEM((NN, 16, 256), BF16),
            pltpu.VMEM((2, 16, 128, 128), BF16),
            pltpu.VMEM((256, 1024), BF16),
            pltpu.VMEM((256, 1024), BF16),
            pltpu.VMEM((256, 1024), BF16),
            pltpu.VMEM((256, 256), BF16),
            pltpu.VMEM((256, 256), BF16),
            pltpu.VMEM((256, 1024), F32),
            pltpu.VMEM((NZ, 128, 128), F32),
            pltpu.VMEM((NZ, 128, 128), BF16),
            pltpu.VMEM((NZ, 128, 128), BF16),
            pltpu.VMEM((NZ, 128, 128), BF16),
            pltpu.VMEM((128, 128), F32),
            pltpu.VMEM((NZ, 128, 128), BF16),
            pltpu.VMEM((512, 256), BF16),
            pltpu.VMEM((512, 512), BF16),
            pltpu.VMEM((4, 256, 256), BF16),
            pltpu.VMEM((4, 256, 256), BF16),
            pltpu.VMEM((4, NX, 64, 256), F32),
            pltpu.VMEM((4, NX - 1, 64, 256), BF16),
            pltpu.VMEM((4, NY, 8, 256), F32),
            pltpu.VMEM((4, NY - 1, 8, 256), F32),
            pltpu.VMEM((8, 8, 128), F32),
            dma((6,)),
            dma,
            dma,
            dma((NZ,)),
            dma((NZ,)),
            dma((NZ,)),
            dma((NZ,)),
            dma((4,)),
            dma((4,)),
            dma((4,)),
            dma((4,)),
            dma((4,)),
            dma((4,)),
        ],
        compiler_params=pltpu.CompilerParams(
            collective_id=0, has_side_effects=True, vmem_limit_bytes=40 * 1024 * 1024
        ),
        name="sage_layer",
    )(
        features.reshape(64, 16, 256), idx, seed_ids.reshape(2, 128), tile_src, tile_weights,
        w_self, w_neigh, cotangent,
    )


def solution(mesh):
    in_specs = (
        P("node", "col"),
        P("node"),
        P("node", None, None),
        P("node", None),
        P("node", None),
        P("node", None, None, None),
        P("col", None),
        P("col", None),
        P("node", None),
    )
    out_specs = (P("node", "col"), P(("col", "node"), None), P(("col", "node"), None))
    return jax.shard_map(
        on_device, mesh=mesh, in_specs=in_specs, out_specs=out_specs, check_vma=False
    )
```

time: 429 us -> 92.3 us (0.22)
  waiting for transfers between devices: 370 us -> 0 us
  Pallas kernels: 0 us -> 80.8 us
  starting transfers between devices: 18.3 us -> 0 us
  between operations: 14.8 us -> 0.67 us
  matrix products: 7.34 us -> 0 us
  other arithmetic: 5.44 us -> 0.67 us
    unnamed x3 -> x0, waiting for transfers between devices: 223 us -> none
    psum x1 -> x0, waiting for transfers between devices: 132 us -> none  [on_device(): full_sum = lax.psum(partial_value, 'col')]
    pallas_call x0 -> x1, Pallas kernels: none -> 80.8 us  [on_device(): pl.pallas_call(kernel, out_shape=(jax.ShapeDtypeStruct((256, 64), BF16),...]
    all_to_all x1 -> x0, starting transfers between devices: 18.2 us -> none  [on_device(): lax.all_to_all(outgoing, 'node', split_axis=0, concat_axis=0, tiled=True)]
    all_to_all x1 -> x0, waiting for transfers between devices: 15.2 us -> none  [on_device(): lax.all_to_all(outgoing, 'node', split_axis=0, concat_axis=0, tiled=True)]
    gather x3 -> x0, local copies, waits for them, and re-layouts: 7.73 us -> none  [the longest x1 4.57 us: on_device(): picked = features[send_rows[0]]]
    dot_general x5 -> x0, matrix products: 7.34 us -> none  [the longest x1 2.15 us: on_device(): jnp.einsum('skij,skjc->sic', tile_weights, blocks, preferred_element_type...]
    unnamed x17 -> x22, local copies, waits for them, and re-layouts: 3.42 us -> 8.63 us
  transfers between devices with their start and end apart: 3 -> 0, of which waited for: 3 -> 0; matrix products, arithmetic and copies ran while one was open for 1% -> 0% of each run, Pallas kernels for 0% -> 0%
where the time goes in v1:
time: 92.3 us; the launch traced here: 91.8 us
  Pallas kernels  80.8 us (88%)
  local copies, waits for them, and re-layouts  9.74 us (11%)
    pallas_call x1, Pallas kernels, on_device(): pl.pallas_call(kernel, out_shape=(jax.ShapeDtypeStruct((256, 64), BF16),...  80.8 us
    unnamed x22, local copies, waits for them, and re-layouts  8.63 us

profile of v1, /device:TPU:1, one launch (start us, length us, event | category | flops | bytes accessed | tf_op | source)
XLA Modules:
  0.0 91.8 jit_solution(12317620377990449367)
XLA Ops:
  0.6 0.0 copy-start.8
  0.6 0.5 broadcast.8
  1.2 0.1 copy-done.8
  1.3 0.7 reduce.3
  2.0 0.1 lt.13
  2.0 0.1 iota.12
  2.1 0.1 lt.14
  2.2 0.0 copy-start.7
  2.2 0.1 lt.15
  2.3 0.6 copy-done.7
  2.9 0.1 copy.14
  3.0 0.1 squeeze.3
  3.1 0.0 copy-start.5
  3.1 0.0 copy-start.6
  3.1 0.7 copy-done.5
  3.7 0.0 copy-done.6
  3.8 0.0 copy-start
  3.8 1.2 %copy-done = bf16[2,16,128,128]{3,2,1,0:T(8,128)(2,1)S(1)} copy-done((bf16[2,16,128,128]{3,2,1,0:T(8,128)(2,1)S(1)}, bf16[2,16,128,128]{3,2,1,0:T(8,128)(2,1)}, u32[]{:S(2)}) %copy-start) | copy-done | bytes 1048600
  5.0 0.0 copy-start.1
  5.0 1.0 %copy-done.1 = bf16[1024,256]{1,0:T(8,128)(2,1)S(1)} copy-done((bf16[1024,256]{1,0:T(8,128)(2,1)S(1)}, bf16[1024,256]{1,0:T(8,128)(2,1)}, u32[]{:S(2)}) %copy-start.1) | copy-done | bytes 524312
  6.0 0.0 copy-start.2
  6.0 1.0 %copy-done.2 = bf16[256,1024]{1,0:T(8,128)(2,1)S(1)} copy-done((bf16[256,1024]{1,0:T(8,128)(2,1)S(1)}, bf16[256,1024]{1,0:T(8,128)(2,1)}, u32[]{:S(2)}) %copy-start.2) | copy-done | bytes 524312
  7.1 0.0 copy-start.3
  7.1 1.0 %copy-done.3 = bf16[256,1024]{1,0:T(8,128)(2,1)S(1)} copy-done((bf16[256,1024]{1,0:T(8,128)(2,1)S(1)}, bf16[256,1024]{1,0:T(8,128)(2,1)}, u32[]{:S(2)}) %copy-start.3) | copy-done | bytes 524312
  8.1 0.0 copy-start.4
  8.1 1.0 %copy-done.4 = bf16[256,1024]{1,0:T(8,128)(2,1)S(1)} copy-done((bf16[256,1024]{1,0:T(8,128)(2,1)S(1)}, bf16[256,1024]{1,0:T(8,128)(2,1)}, u32[]{:S(2)}) %copy-start.4) | copy-done | bytes 524312
  9.2 80.8 %sage_layer.1 = (bf16[256,64]{1,0:T(8,128)(2,1)S(1)}, f32[4,1024]{1,0:T(4,128)S(1)}, f32[4,1024]{1,0:T(4,128)S(1)}) custom-call(bf16[64,16,256]{2,1,0:T(8,128)(2,1)S(1)} %bitcast.2, s32[8,128]{1,0:T(8,128)S(1)} %compare_select_fusion.idx, s32[2,128]{1,0:T(2,128)S(1)} %bitcast.3, s32[2,16]{1,0:T(2,128)S(1)} %copy-done.6, ...), custom_call_target="tpu_custom_call" | custom-call | tf_op jit(solution)/shard_map/sage_layer/pallas_call | solution.py:353
  89.9 0.7 copy.15
  90.6 0.6 copy.18
  91.2 0.6 copy.19
  (2 shorter events, 0.0 us)
Async XLA Ops:
  0.6 0.7 copy-start.8
  2.2 0.7 copy-start.7
  3.1 0.7 copy-start.5
  3.1 0.7 copy-start.6
  3.8 1.2 %copy-start = (bf16[2,16,128,128]{3,2,1,0:T(8,128)(2,1)S(1)}, bf16[2,16,128,128]{3,2,1,0:T(8,128)(2,1)}, u32[]{:S(2)}) copy-start(bf16[2,16,128,128]{3,2,1,0:T(8,128)(2,1)} %tw_hbm.1) | copy-start | bytes 3145732
  5.0 1.0 %copy-start.1 = (bf16[1024,256]{1,0:T(8,128)(2,1)S(1)}, bf16[1024,256]{1,0:T(8,128)(2,1)}, u32[]{:S(2)}) copy-start(bf16[1024,256]{1,0:T(8,128)(2,1)} %param.9) | copy-start | bytes 1572868
  6.0 1.0 %copy-start.2 = (bf16[256,1024]{1,0:T(8,128)(2,1)S(1)}, bf16[256,1024]{1,0:T(8,128)(2,1)}, u32[]{:S(2)}) copy-start(bf16[256,1024]{1,0:T(8,128)(2,1)} %ws_hbm.1) | copy-start | bytes 1572868
  7.1 1.0 %copy-start.3 = (bf16[256,1024]{1,0:T(8,128)(2,1)S(1)}, bf16[256,1024]{1,0:T(8,128)(2,1)}, u32[]{:S(2)}) copy-start(bf16[256,1024]{1,0:T(8,128)(2,1)} %wn_hbm.1) | copy-start | bytes 1572868
  8.1 1.0 %copy-start.4 = (bf16[256,1024]{1,0:T(8,128)(2,1)S(1)}, bf16[256,1024]{1,0:T(8,128)(2,1)}, u32[]{:S(2)}) copy-start(bf16[256,1024]{1,0:T(8,128)(2,1)} %cot_hbm.1) | copy-start | bytes 1572868

commit v2 on v1

--- a/solution.py
+++ b/solution.py
@@ -11,6 +11,7 @@
 
 NZ, NY, NX, NC = 16, 8, 4, 2
 NN = NY * NX * NC
+NBAR = NN - 1 + 6
 
 PARENT = {
     8: 6, 7: 6, 5: 6, -7: -6, -5: -6, 6: 3, -6: -3,
@@ -28,8 +29,7 @@
     return lax.broadcasted_iota(jnp.int32, shape, 1) < 64
 
 
-def one_hot_rows(row):
-    spread = jnp.broadcast_to(row.astype(F32), (128, 128)).T
+def one_hot_rows(spread):
     lane = lax.broadcasted_iota(jnp.int32, (128, 128), 1).astype(F32)
     parts = [
         jnp.where(spread == lane + 128.0 * j, 1.0, 0.0).astype(BF16) for j in range(8)
@@ -38,10 +38,10 @@
 
 
 def kernel(
-    feat, idx, seed, tsrc, tw_hbm, ws_hbm, wn_hbm, cot_hbm,
-    hid, gs, gn,
-    src, out, tw, ws, wn, cot, sf, nm, part, pk, pkb, rb, sb, cp, ag, xpt, stack,
-    cs, cr, xs, xr, ys, yr, fin,
+    feat, rows_hbm, counts_hbm, seed_hbm, tsrc_hbm, tw_hbm, ws_hbm, wn_hbm, cot_hbm,
+    hid, grads,
+    rows, counts, seed, tsrc, slots, src, out, tw, ws, wn, cot, sf, nm, part, pk, pkb, rb, sb, cp, ag, xpt, stack,
+    cs, cr, xs, xb, xr, lx, lb, lr, ys, yb, yr, fin,
     lsem, a_send, a_recv, b_send, b_recv, c_send, c_recv,
     dc_send, dc_recv, dx_send, dx_recv, dy_send, dy_recv,
 ):
@@ -57,29 +57,44 @@
     loads = [
         pltpu.make_async_copy(a, b, lsem.at[i])
         for i, (a, b) in enumerate((
-            (feat, src.at[pl.ds(0, NN)]), (ws_hbm, ws), (tw_hbm, tw), (wn_hbm, wn), (cot_hbm, cot),
+            (rows_hbm, rows), (counts_hbm, counts), (feat, src.at[pl.ds(0, NN)]), (seed_hbm, seed),
+            (ws_hbm, ws), (cot_hbm, cot), (tsrc_hbm, tsrc), (tw_hbm, tw), (wn_hbm, wn),
         ))
     ]
-    for load in loads:
+    for load in loads[:3]:
         load.start()
 
     barrier = pltpu.get_barrier_semaphore()
-
-    @pl.loop(1, NN)
-    def _(k):
-        pl.semaphore_signal(
-            barrier, inc=1, device_id=(z, (node + k) % NN), device_id_type=MESH
-        )
-
-    for d in (1, -1, 2, -2, 3, -3):
+    for d in (4, 3, 5, 2, 6, 1, 7, 0):
+        for j in range(8):
+            if d or j:
+                to = ((y + d) % NY) * 8 + (node + j) % 8
+                pl.semaphore_signal(barrier, inc=1, device_id=(z, to), device_id_type=MESH)
+    for d in (3, -3, 2, -2, 1, -1):
         pl.semaphore_signal(barrier, inc=1, device_id=(zat(d), node), device_id_type=MESH)
+    for load in loads[3:]:
+        load.start()
+
     loads[0].wait()
+    loads[1].wait()
+    live = lax.broadcasted_iota(jnp.int32, (16, 64), 0) < counts[...]
+    table = jnp.where(live, rows[...], -1).astype(F32)
+    table = jnp.concatenate([table, jnp.zeros((16, 64), F32)], axis=1)
+    slots[...] = jnp.concatenate([table, jnp.zeros((112, 128), F32)], axis=0).T
+    loads[2].wait()
     feats = src[pl.ds(0, NN)].reshape(1024, 256)
+    own_slot = (
+        lax.broadcasted_iota(jnp.int32, (128, 128), 0) % 16
+        == lax.broadcasted_iota(jnp.int32, (128, 128), 1)
+    )
 
     def gather(yy):
-        hot = one_hot_rows(idx[pl.ds(yy, 1), :])
-        rows = jnp.dot(hot, feats, preferred_element_type=F32).astype(BF16)
-        out[pl.ds(pl.multiple_of(yy * 8, 8), 8)] = rows.reshape(8, 16, 256)
+        tile = slots[pl.ds(pl.multiple_of(yy * 8, 8), 8), :]
+        tile = jnp.broadcast_to(tile[:, None, :], (8, 16, 128)).reshape(128, 128)
+        spread = jnp.sum(jnp.where(own_slot, tile, 0.0), axis=1, keepdims=True)
+        hot = one_hot_rows(spread)
+        picked = jnp.dot(hot, feats, preferred_element_type=F32).astype(BF16)
+        out[pl.ds(pl.multiple_of(yy * 8, 8), 8)] = picked.reshape(8, 16, 256)
 
     def send_rows(to):
         pltpu.make_async_remote_copy(
@@ -91,19 +106,20 @@
         yy = (y + d) % NY
         gather(yy)
         if step == 0:
-            pl.semaphore_wait(barrier, NN - 1 + 6)
+            pl.semaphore_wait(barrier, NBAR)
         for j in range(8):
-            send_rows(yy * 8 + j)
+            send_rows(yy * 8 + (node + j) % 8)
     gather(y)
     for j in range(1, 8):
         send_rows(y * 8 + (node + j) % 8)
-    own = pltpu.make_async_copy(out.at[node], src.at[NN + node], lsem.at[5])
+    own = pltpu.make_async_copy(out.at[node], src.at[NN + node], lsem.at[9])
     own.start()
 
+    loads[3].wait()
     for b in range(2):
-        hot = one_hot_rows(seed[pl.ds(b, 1), :])
+        hot = one_hot_rows(jnp.broadcast_to(seed[b:b + 1, :].astype(F32), (128, 128)).T)
         sf[pl.ds(b * 128, 128), :] = jnp.dot(hot, feats, preferred_element_type=F32).astype(BF16)
-    loads[1].wait()
+    loads[4].wait()
     part[...] = jnp.dot(sf[...], ws[...], preferred_element_type=F32)
 
     r = lax.broadcasted_iota(jnp.int32, (512, 512), 0)
@@ -116,7 +132,7 @@
     stack[...] = perm
     nt = (((1,), (1,)), ((), ()))
 
-    loads[4].wait()
+    loads[5].wait()
     pair = pl.ds(pl.multiple_of((z // 2) * 128, 128), 128)
     c0 = cot[0:128, pair].astype(F32)
     c1 = cot[128:256, pair].astype(F32)
@@ -127,8 +143,8 @@
         jnp.where(even, c0, pltpu.roll(c0, 64, 1)),
         jnp.where(even, pltpu.roll(c1, 64, 1), c1),
     )
-    loads[2].wait()
-    loads[3].wait()
+    for load in loads[6:]:
+        load.wait()
 
     own.wait()
     pltpu.make_async_remote_copy(
@@ -144,16 +160,6 @@
             )
             total += jnp.dot(weight, block, preferred_element_type=F32)
         nm[pl.ds(b * 128, 128), :] = total.astype(BF16)
-    for p in range(8):
-        cols = pl.ds(p * 128, 128)
-        value = part[:, cols] + jnp.dot(nm[...], wn[:, cols], preferred_element_type=F32)
-        p0, p1 = value[0:128], value[128:256]
-        first = jnp.where(left, p0, pltpu.roll(p1, 64, 1))
-        second = jnp.where(left, pltpu.roll(p0, 64, 1), p1)
-        pk[2 * p] = first
-        pk[2 * p + 1] = second
-        pkb[2 * p] = first.astype(BF16)
-        pkb[2 * p + 1] = second.astype(BF16)
 
     def up(o, source):
         return pltpu.make_async_remote_copy(
@@ -163,8 +169,20 @@
         )
 
     ups = {o: up(o, pkb.at[zat(-o)]) for o in LEAVES}
-    for o in LEAVES:
-        ups[o].start()
+    for pairs, leaves in (((4, 3, -3), (8, 7, -7)), ((2, -2), (5, -5, 4, -4)), ((1, -1, 0), (2, -2, 1, -1))):
+        for q in pairs:
+            p = (z // 2 + q + 8) % 8
+            cols = pl.ds(pl.multiple_of(p * 128, 128), 128)
+            value = part[:, cols] + jnp.dot(nm[...], wn[:, cols], preferred_element_type=F32)
+            p0, p1 = value[0:128], value[128:256]
+            first = jnp.where(left, p0, pltpu.roll(p1, 64, 1))
+            second = jnp.where(left, pltpu.roll(p0, 64, 1), p1)
+            pk[2 * p] = first
+            pk[2 * p + 1] = second
+            pkb[2 * p] = first.astype(BF16)
+            pkb[2 * p + 1] = second.astype(BF16)
+        for o in leaves:
+            ups[o].start()
 
     xpt[...] = (
         lax.dot_general(stack[:, 0:256], sf[...], nt, preferred_element_type=F32)
@@ -208,14 +226,15 @@
 
     forward(3, -3, 1, -1)
     value = pre * s
-    hid[0:128, :] = value[:, 0:64].astype(BF16)
-    hid[128:256, :] = pltpu.roll(value, 64, 1)[:, 0:64].astype(BF16)
+    value = value.T
+    hid[:, 0:128] = value[0:64].astype(BF16)
+    hid[:, 128:256] = value[64:128].astype(BF16)
 
     own_rows = pl.ds(pl.multiple_of(core * 256, 256), 256)
     other_rows = pl.ds(pl.multiple_of((1 - core) * 256, 256), 256)
     kept, copies = {}, {}
 
-    def terms(g):
+    def gathered(g):
         halves = []
         for q in (0, 2):
             a = ag[slot(GROUPS[g][q])].astype(F32)
@@ -226,37 +245,50 @@
                     jnp.where(left, pltpu.roll(a, 64, 1), b),
                 ], axis=0,
             ).astype(BF16))
-        grad = jnp.concatenate(halves, axis=1)
+        return jnp.concatenate(halves, axis=1)
+
+    def terms(g):
+        grad = gathered(g)
         cs[g] = jnp.dot(xpt[other_rows, :], grad, preferred_element_type=F32).astype(BF16)
-        copies["c", g] = pltpu.make_async_remote_copy(
+        copies[g] = pltpu.make_async_remote_copy(
             src_ref=cs.at[g], dst_ref=cr.at[g], send_sem=dc_send.at[g], recv_sem=dc_recv.at[g],
             device_id=(z, node + 1 - 2 * core), device_id_type=MESH,
         )
-        copies["c", g].start()
+        copies[g].start()
         kept[g] = jnp.dot(xpt[own_rows, :], grad, preferred_element_type=F32)
 
-    def over_x(g):
-        copies["c", g].wait_recv()
+    def start_x(g):
+        copies[g].wait_recv()
         total = kept[g] + cr[g].astype(F32)
-        for xx in range(4):
-            xs[g, xx] = total[xx * 64:(xx + 1) * 64]
-        for xx in range(4):
-            cs[g, pl.ds(xx * 64, 64)] = total[xx * 64:(xx + 1) * 64].astype(BF16)
-
-    def start_x(g):
-        copies["c", g].wait_send()
-        over_x(g)
-        for i in range(1, NX):
+        xs[g] = total
+        xb[g] = total.astype(BF16)
+        for i in (2, 1, 3):
             to = (x + i) % NX
             pltpu.make_async_remote_copy(
-                src_ref=cs.at[g, pl.ds(pl.multiple_of(to * 64, 64), 64)], dst_ref=xr.at[g, i - 1],
+                src_ref=xb.at[g, pl.ds(pl.multiple_of(to * 64, 64), 64)], dst_ref=xr.at[g, i - 1],
                 send_sem=dx_send.at[g], recv_sem=dx_recv.at[g],
                 device_id=(z, (y * NX + to) * NC + core), device_id_type=MESH,
             ).start()
 
+    last = len(GROUPS) - 1
+
+    def last_terms():
+        total = jnp.dot(xpt[...], gathered(last), preferred_element_type=F32)
+        lb[...] = total.astype(BF16)
+        for i in (4, 5, 3, 2, 6, 1, 7):
+            to = (node + i) % 8
+            rows_to = (to % NC) * 256 + (to // NC) * 64
+            pltpu.make_async_remote_copy(
+                src_ref=lb.at[pl.ds(pl.multiple_of(rows_to, 64), 64)], dst_ref=lr.at[i - 1],
+                send_sem=dx_send.at[last], recv_sem=dx_recv.at[last],
+                device_id=(z, y * 8 + to), device_id_type=MESH,
+            ).start()
+        lx[...] = total
+
     def all_x(g):
+        ref = lr if g == last else xr.at[g]
         return pltpu.make_async_remote_copy(
-            src_ref=xr.at[g], dst_ref=xr.at[g], send_sem=dx_send.at[g], recv_sem=dx_recv.at[g],
+            src_ref=ref, dst_ref=ref, send_sem=dx_send.at[g], recv_sem=dx_recv.at[g],
             device_id=(z, node), device_id_type=MESH,
         )
 
@@ -268,14 +300,22 @@
 
     def start_y(g):
         all_x(g).wait_recv()
-        total = xs[g, x]
-        for i in range(NX - 1):
-            total = total + xr[g, i].astype(F32)
-        ys[g] = total.reshape(NY, 8, 256)
+        if g == last:
+            total = lx[pl.ds(pl.multiple_of(core * 256 + x * 64, 64), 64), :]
+            for i in range(7):
+                total = total + lr[i].astype(F32)
+        else:
+            total = xs[g, pl.ds(pl.multiple_of(x * 64, 64), 64), :]
+            for i in range(NX - 1):
+                total = total + xr[g, i].astype(F32)
+        total = total.reshape(NY, 8, 256)
+        total = jnp.concatenate([total[:, :, 0:128], total[:, :, 128:256]], axis=1)
+        ys[g] = total
+        yb[g] = total.astype(BF16)
         for i in (4, 3, 5, 2, 6, 1, 7):
             to = (y + i) % NY
             pltpu.make_async_remote_copy(
-                src_ref=ys.at[g, to], dst_ref=yr.at[g, i - 1],
+                src_ref=yb.at[g, to], dst_ref=yr.at[g, i - 1],
                 send_sem=dy_send.at[g], recv_sem=dy_recv.at[g],
                 device_id=(z, (to * NX + x) * NC + core), device_id_type=MESH,
             ).start()
@@ -286,11 +326,11 @@
         all_y(g).wait_recv()
         total = ys[g, y]
         for i in range(NY - 1):
-            total = total + yr[g, i]
+            total = total + yr[g, i].astype(F32)
         for q in range(4):
             chunk = zat(-GROUPS[g][q])
             side = chunk % 2
-            tile = total[:, (q // 2) * 128:(q // 2 + 1) * 128]
+            tile = total[(q // 2) * 8:(q // 2 + 1) * 8]
             tile = jnp.where(side == q % 2, tile, pltpu.roll(tile, 64, 1))
             fin[chunk // 2] = jnp.where(half == side, tile, fin[chunk // 2])
 
@@ -313,10 +353,9 @@
     start_x(1)
     start_y(0)
     arrived(7, -5, -7, 8)
-    terms(3)
+    last_terms()
     start_x(2)
     start_y(1)
-    start_x(3)
     start_y(2)
     finish(0)
     start_y(3)
@@ -325,8 +364,7 @@
     finish(3)
     for p in range(8):
         cols = pl.ds(p * 128, 128)
-        gs[:, cols] = fin[p, 0:4, :]
-        gn[:, cols] = fin[p, 4:8, :]
+        grads[:, cols] = fin[p]
 
     pltpu.make_async_remote_copy(
         src_ref=out.at[pl.ds(0, NN - 1)], dst_ref=out.at[pl.ds(0, NN - 1)],
@@ -336,30 +374,44 @@
         ups[o].wait_send()
         downs[o].wait_send()
     for g in range(4):
+        if g != last:
+            copies[g].wait_send()
         all_x(g).wait_send()
         all_y(g).wait_send()
+
+
+def write_out(hidden, grads, hid, grad_self, grad_neigh, sems):
+    copies = [
+        pltpu.make_async_copy(hidden, hid, sems.at[0]),
+        pltpu.make_async_copy(grads.at[0:4], grad_self, sems.at[1]),
+        pltpu.make_async_copy(grads.at[4:8], grad_neigh, sems.at[2]),
+    ]
+    for copy in copies:
+        copy.start()
+    for copy in copies:
+        copy.wait()
 
 
 def on_device(
     features, seed_ids, send_rows, send_counts, tile_src, tile_weights, w_self, w_neigh, cotangent
 ):
-    slot_ids = lax.broadcasted_iota(jnp.int32, send_rows.shape[1:], 1)
-    live = slot_ids < send_counts[0][:, None]
-    idx = jnp.where(live, send_rows[0], -1).reshape(8, 128)
-    any_space = pl.BlockSpec(memory_space=pl.ANY)
+    hbm = pl.BlockSpec(memory_space=pltpu.HBM)
     vmem = pl.BlockSpec(memory_space=pltpu.VMEM)
-    smem = pl.BlockSpec(memory_space=pltpu.SMEM)
     dma = pltpu.SemaphoreType.DMA
-    return pl.pallas_call(
+    hidden_t, grads = pl.pallas_call(
         kernel,
         out_shape=(
-            jax.ShapeDtypeStruct((256, 64), BF16),
-            jax.ShapeDtypeStruct((4, 1024), F32),
-            jax.ShapeDtypeStruct((4, 1024), F32),
+            jax.ShapeDtypeStruct((64, 256), BF16),
+            jax.ShapeDtypeStruct((8, 1024), F32),
         ),
-        in_specs=[any_space, vmem, vmem, smem, any_space, any_space, any_space, any_space],
-        out_specs=(vmem, vmem, vmem),
+        in_specs=[hbm] * 9,
+        out_specs=(vmem, vmem),
         scratch_shapes=[
+            pltpu.VMEM((16, 64), jnp.int32),
+            pltpu.VMEM((1, 64), jnp.int32),
+            pltpu.VMEM((2, 128), jnp.int32),
+            pltpu.SMEM((2, 16), jnp.int32),
+            pltpu.VMEM((128, 128), F32),
             pltpu.VMEM((2 * NN, 16, 256), BF16),
             pltpu.VMEM((NN, 16, 256), BF16),
             pltpu.VMEM((2, 16, 128, 128), BF16),
@@ -377,35 +429,53 @@
             pltpu.VMEM((NZ, 128, 128), BF16),
             pltpu.VMEM((512, 256), BF16),
             pltpu.VMEM((512, 512), BF16),
-            pltpu.VMEM((4, 256, 256), BF16),
-            pltpu.VMEM((4, 256, 256), BF16),
-            pltpu.VMEM((4, NX, 64, 256), F32),
-            pltpu.VMEM((4, NX - 1, 64, 256), BF16),
-            pltpu.VMEM((4, NY, 8, 256), F32),
-            pltpu.VMEM((4, NY - 1, 8, 256), F32),
+            pltpu.VMEM((3, 256, 256), BF16),
+            pltpu.VMEM((3, 256, 256), BF16),
+            pltpu.VMEM((3, 256, 256), F32),
+            pltpu.VMEM((3, 256, 256), BF16),
+            pltpu.VMEM((3, NX - 1, 64, 256), BF16),
+            pltpu.VMEM((512, 256), F32),
+            pltpu.VMEM((512, 256), BF16),
+            pltpu.VMEM((7, 64, 256), BF16),
+            pltpu.VMEM((4, NY, 16, 128), F32),
+            pltpu.VMEM((4, NY, 16, 128), BF16),
+            pltpu.VMEM((4, NY - 1, 16, 128), BF16),
             pltpu.VMEM((8, 8, 128), F32),
-            dma((6,)),
+            dma((10,)),
             dma,
             dma,
             dma((NZ,)),
             dma((NZ,)),
             dma((NZ,)),
             dma((NZ,)),
-            dma((4,)),
-            dma((4,)),
+            dma((3,)),
+            dma((3,)),
             dma((4,)),
             dma((4,)),
             dma((4,)),
             dma((4,)),
         ],
         compiler_params=pltpu.CompilerParams(
-            collective_id=0, has_side_effects=True, vmem_limit_bytes=40 * 1024 * 1024
+            collective_id=0, has_side_effects=True, vmem_limit_bytes=60 * 1024 * 1024
         ),
         name="sage_layer",
     )(
-        features.reshape(64, 16, 256), idx, seed_ids.reshape(2, 128), tile_src, tile_weights,
-        w_self, w_neigh, cotangent,
-    )
+        features.reshape(64, 16, 256), send_rows[0].T, send_counts, seed_ids.reshape(2, 128),
+        tile_src, tile_weights, w_self, w_neigh, cotangent,
+    )
+    hidden_t, grad_self, grad_neigh = pl.pallas_call(
+        write_out,
+        out_shape=(
+            jax.ShapeDtypeStruct((64, 256), BF16),
+            jax.ShapeDtypeStruct((4, 1024), F32),
+            jax.ShapeDtypeStruct((4, 1024), F32),
+        ),
+        in_specs=[vmem] * 2,
+        out_specs=(hbm,) * 3,
+        scratch_shapes=[dma((3,))],
+        name="write_out",
+    )(hidden_t, grads)
+    return hidden_t.T, grad_self, grad_neigh
 
 
 def solution(mesh):

time: 92.3 us -> 82.3 us (0.89)
  local copies, waits for them, and re-layouts: 9.74 us -> 0 us
    unnamed x22 -> x0, local copies, waits for them, and re-layouts: 8.63 us -> none
    pallas_call x1 -> x2, Pallas kernels: 80.8 us -> 80.9 us  [the longest x1 79.5 us: on_device(): pl.pallas_call(kernel, out_shape=(jax.ShapeDtypeStruct((64, 256), BF16),...]
where the time goes in v2:
time: 82.3 us; the launch traced here: 81.5 us
  Pallas kernels  80.9 us (98%)
    pallas_call x1, Pallas kernels, on_device(): pl.pallas_call(kernel, out_shape=(jax.ShapeDtypeStruct((64, 256), BF16),...  79.5 us

profile of v2, /device:TPU:1, one launch (start us, length us, event | category | flops | bytes accessed | tf_op | source)
XLA Modules:
  0.0 81.5 jit_solution(9500449274983858552)
XLA Ops:
  0.6 79.5 %sage_layer.1 = (bf16[64,256]{1,0:T(8,128)(2,1)}, f32[8,1024]{1,0:T(8,128)}) custom-call(bf16[64,16,256]{2,1,0:T(8,128)(2,1)} %bitcast.6, s32[16,64]{1,0:T(8,128)} %bitcast.7, s32[1,64]{1,0:T(1,128)} %counts_hbm.1, s32[2,128]{1,0:T(2,128)} %bitcast.8, s32[2,16]{1,0:T(2,128)} %tsrc_hbm.1, bf16[2,16,128,128]{3,2,1,0:T(8,128)(2,1)} %tw_hbm.1, ...), custom_call_target="tpu_custom_call" | custom-call | tf_op jit(solution)/shard_map/sage_layer/pallas_call | solution.py:401
  80.1 1.4 %write_out.1 = (bf16[64,256]{1,0:T(8,128)(2,1)}, f32[4,1024]{1,0:T(4,128)}, f32[4,1024]{1,0:T(4,128)}) custom-call(bf16[64,256]{1,0:T(8,128)(2,1)} %get-tuple-element.8.hidden, f32[8,1024]{1,0:T(8,128)} %get-tuple-element.9.grads), custom_call_target="tpu_custom_call" | custom-call | tf_op jit(solution)/shard_map/write_out/pallas_call | solution.py:466

commit v3 on v2

--- a/solution.py
+++ b/solution.py
@@ -14,15 +14,24 @@
 NBAR = NN - 1 + 6
 
 PARENT = {
-    8: 6, 7: 6, 5: 6, -7: -6, -5: -6, 6: 3, -6: -3,
+    8: 6, -8: -6, 7: 6, 5: 6, -7: -6, -5: -6, 6: 3, -6: -3,
     4: 3, 2: 3, -4: -3, -2: -3, 3: 0, -3: 0, 1: 0, -1: 0,
 }
-LEAVES = (8, 7, -7, 5, -5, 4, -4, 2, -2, 1, -1)
+LEAVES = (8, -8, 7, -7, 5, -5, 4, -4, 2, -2, 1, -1)
+HALVES = {8: 0, -8: 64}
 GROUPS = ((0, 1, -1, 3), (-3, 2, -2, 4), (-4, 6, -6, 5), (7, -5, -7, 8))
 
 
 def slot(offset):
     return offset % NZ
+
+
+def sem(offset):
+    return 0 if offset == -8 else slot(offset)
+
+
+def rows_of(ref, offset):
+    return ref.at[pl.ds(HALVES[offset], 64)] if offset in HALVES else ref
 
 
 def left_half(shape):
@@ -41,7 +50,7 @@
     feat, rows_hbm, counts_hbm, seed_hbm, tsrc_hbm, tw_hbm, ws_hbm, wn_hbm, cot_hbm,
     hid, grads,
     rows, counts, seed, tsrc, slots, src, out, tw, ws, wn, cot, sf, nm, part, pk, pkb, rb, sb, cp, ag, xpt, stack,
-    cs, cr, xs, xb, xr, lx, lb, lr, ys, yb, yr, fin,
+    cs, cr, xs, xb, xr, ys, yb, yr, fin,
     lsem, a_send, a_recv, b_send, b_recv, c_send, c_recv,
     dc_send, dc_recv, dx_send, dx_recv, dy_send, dy_recv,
 ):
@@ -163,13 +172,13 @@
 
     def up(o, source):
         return pltpu.make_async_remote_copy(
-            src_ref=source, dst_ref=rb.at[slot(o)],
-            send_sem=b_send.at[slot(o)], recv_sem=b_recv.at[slot(o)],
+            src_ref=rows_of(source, o), dst_ref=rows_of(rb.at[slot(o)], o),
+            send_sem=b_send.at[sem(o)], recv_sem=b_recv.at[sem(o)],
             device_id=(zat(PARENT[o] - o), node), device_id_type=MESH,
         )
 
     ups = {o: up(o, pkb.at[zat(-o)]) for o in LEAVES}
-    for pairs, leaves in (((4, 3, -3), (8, 7, -7)), ((2, -2), (5, -5, 4, -4)), ((1, -1, 0), (2, -2, 1, -1))):
+    for pairs, leaves in (((4, 3, -3), (8, -8, 7, -7)), ((2, -2), (5, -5)), ((1, -1, 0), ())):
         for q in pairs:
             p = (z // 2 + q + 8) % 8
             cols = pl.ds(pl.multiple_of(p * 128, 128), 128)
@@ -189,17 +198,36 @@
         + lax.dot_general(stack[:, 256:512], nm[...], nt, preferred_element_type=F32)
     ).astype(BF16)
 
+    for o in (4, -4, 2, -2):
+        ups[o].start()
+
     def summed(o, children):
         value = pk[zat(-o)]
         for child in children:
             ups[child].wait_recv()
-            value = value + rb[slot(child)].astype(F32)
+            if child == 8:
+                here, rest = value[0:64], value[64:128]
+                here = here + rb[slot(8), 0:64].astype(F32)
+                value = jnp.concatenate([here, rest], axis=0)
+            elif child == -8:
+                rest, here = value[0:64], value[64:128]
+                here = here + rb[slot(8), 64:128].astype(F32)
+                value = jnp.concatenate([rest, here], axis=0)
+            else:
+                value = value + rb[slot(child)].astype(F32)
         return value
 
-    for o, children in ((6, (7, 5, 8)), (-6, (-7, -5)), (3, (4, 2, 6)), (-3, (-4, -2, -6))):
+    def hand_up(o, children):
         sb[slot(o)] = summed(o, children).astype(BF16)
         ups[o] = up(o, sb.at[slot(o)])
         ups[o].start()
+
+    hand_up(6, (7, 8, 5))
+    hand_up(-6, (-7, -8, -5))
+    ups[1].start()
+    ups[-1].start()
+    hand_up(3, (4, 2, 6))
+    hand_up(-3, (-4, -2, -6))
     pre = summed(0, (1, -1, 3, -3))
 
     s = jax.nn.sigmoid(pre)
@@ -208,8 +236,8 @@
 
     def down(o):
         return pltpu.make_async_remote_copy(
-            src_ref=ag.at[slot(PARENT[o])], dst_ref=ag.at[slot(o)],
-            send_sem=c_send.at[slot(o)], recv_sem=c_recv.at[slot(o)],
+            src_ref=rows_of(ag.at[slot(PARENT[o])], o), dst_ref=rows_of(ag.at[slot(o)], o),
+            send_sem=c_send.at[sem(o)], recv_sem=c_recv.at[sem(o)],
             device_id=(zat(o - PARENT[o]), node), device_id_type=MESH,
         )
 
@@ -224,7 +252,7 @@
         for o in offsets:
             downs[o].wait_recv()
 
-    forward(3, -3, 1, -1)
+    forward(3, -3)
     value = pre * s
     value = value.T
     hid[:, 0:128] = value[0:64].astype(BF16)
@@ -270,25 +298,9 @@
                 device_id=(z, (y * NX + to) * NC + core), device_id_type=MESH,
             ).start()
 
-    last = len(GROUPS) - 1
-
-    def last_terms():
-        total = jnp.dot(xpt[...], gathered(last), preferred_element_type=F32)
-        lb[...] = total.astype(BF16)
-        for i in (4, 5, 3, 2, 6, 1, 7):
-            to = (node + i) % 8
-            rows_to = (to % NC) * 256 + (to // NC) * 64
-            pltpu.make_async_remote_copy(
-                src_ref=lb.at[pl.ds(pl.multiple_of(rows_to, 64), 64)], dst_ref=lr.at[i - 1],
-                send_sem=dx_send.at[last], recv_sem=dx_recv.at[last],
-                device_id=(z, y * 8 + to), device_id_type=MESH,
-            ).start()
-        lx[...] = total
-
     def all_x(g):
-        ref = lr if g == last else xr.at[g]
         return pltpu.make_async_remote_copy(
-            src_ref=ref, dst_ref=ref, send_sem=dx_send.at[g], recv_sem=dx_recv.at[g],
+            src_ref=xr.at[g], dst_ref=xr.at[g], send_sem=dx_send.at[g], recv_sem=dx_recv.at[g],
             device_id=(z, node), device_id_type=MESH,
         )
 
@@ -300,14 +312,9 @@
 
     def start_y(g):
         all_x(g).wait_recv()
-        if g == last:
-            total = lx[pl.ds(pl.multiple_of(core * 256 + x * 64, 64), 64), :]
-            for i in range(7):
-                total = total + lr[i].astype(F32)
-        else:
-            total = xs[g, pl.ds(pl.multiple_of(x * 64, 64), 64), :]
-            for i in range(NX - 1):
-                total = total + xr[g, i].astype(F32)
+        total = xs[g, pl.ds(pl.multiple_of(x * 64, 64), 64), :]
+        for i in range(NX - 1):
+            total = total + xr[g, i].astype(F32)
         total = total.reshape(NY, 8, 256)
         total = jnp.concatenate([total[:, :, 0:128], total[:, :, 128:256]], axis=1)
         ys[g] = total
@@ -335,30 +342,33 @@
             fin[chunk // 2] = jnp.where(half == side, tile, fin[chunk // 2])
 
     fin[...] = jnp.zeros_like(fin)
+    forward(1, -1)
     arrived(3)
-    forward(6, 4, 2)
+    forward(6)
     arrived(-3)
-    forward(-6, -4, -2)
+    forward(-6)
     arrived(1, -1)
     terms(0)
+    forward(4, 2, -4, -2)
+    start_x(0)
     arrived(6)
     forward(8, 7, 5)
     arrived(-6)
-    forward(-7, -5)
+    forward(-8, -7, -5)
     arrived(2, -2, 4)
     terms(1)
-    start_x(0)
     arrived(-4, 5)
     terms(2)
     start_x(1)
+    arrived(7, -5, -7, 8, -8)
+    terms(3)
+    start_x(2)
     start_y(0)
-    arrived(7, -5, -7, 8)
-    last_terms()
-    start_x(2)
+    start_x(3)
     start_y(1)
     start_y(2)
+    start_y(3)
     finish(0)
-    start_y(3)
     finish(1)
     finish(2)
     finish(3)
@@ -374,8 +384,7 @@
         ups[o].wait_send()
         downs[o].wait_send()
     for g in range(4):
-        if g != last:
-            copies[g].wait_send()
+        copies[g].wait_send()
         all_x(g).wait_send()
         all_y(g).wait_send()
 
@@ -429,14 +438,11 @@
             pltpu.VMEM((NZ, 128, 128), BF16),
             pltpu.VMEM((512, 256), BF16),
             pltpu.VMEM((512, 512), BF16),
-            pltpu.VMEM((3, 256, 256), BF16),
-            pltpu.VMEM((3, 256, 256), BF16),
-            pltpu.VMEM((3, 256, 256), F32),
-            pltpu.VMEM((3, 256, 256), BF16),
-            pltpu.VMEM((3, NX - 1, 64, 256), BF16),
-            pltpu.VMEM((512, 256), F32),
-            pltpu.VMEM((512, 256), BF16),
-            pltpu.VMEM((7, 64, 256), BF16),
+            pltpu.VMEM((4, 256, 256), BF16),
+            pltpu.VMEM((4, 256, 256), BF16),
+            pltpu.VMEM((4, 256, 256), F32),
+            pltpu.VMEM((4, 256, 256), BF16),
+            pltpu.VMEM((4, NX - 1, 64, 256), BF16),
             pltpu.VMEM((4, NY, 16, 128), F32),
             pltpu.VMEM((4, NY, 16, 128), BF16),
             pltpu.VMEM((4, NY - 1, 16, 128), BF16),
@@ -448,8 +454,8 @@
             dma((NZ,)),
             dma((NZ,)),
             dma((NZ,)),
-            dma((3,)),
-            dma((3,)),
+            dma((4,)),
+            dma((4,)),
             dma((4,)),
             dma((4,)),
             dma((4,)),

time: 82.3 us -> 80.2 us (0.974)
  Pallas kernels: 80.9 us -> 79.3 us
    pallas_call x1, Pallas kernels: 79.5 us -> 77.9 us  [on_device(): pl.pallas_call(kernel, out_shape=(jax.ShapeDtypeStruct((64, 256), BF16),...]
where the time goes in v3:
time: 80.2 us; the launch traced here: 80 us
  Pallas kernels  79.3 us (99%)
    pallas_call x1, Pallas kernels, on_device(): pl.pallas_call(kernel, out_shape=(jax.ShapeDtypeStruct((64, 256), BF16),...  77.9 us

profile of v3, /device:TPU:1, one launch (start us, length us, event | category | flops | bytes accessed | tf_op | source)
XLA Modules:
  0.0 80.0 jit_solution(18371444898170028207)
XLA Ops:
  0.6 77.9 %sage_layer.1 = (bf16[64,256]{1,0:T(8,128)(2,1)}, f32[8,1024]{1,0:T(8,128)}) custom-call(bf16[64,16,256]{2,1,0:T(8,128)(2,1)} %bitcast.6, s32[16,64]{1,0:T(8,128)} %bitcast.7, s32[1,64]{1,0:T(1,128)} %counts_hbm.1, s32[2,128]{1,0:T(2,128)} %bitcast.8, s32[2,16]{1,0:T(2,128)} %tsrc_hbm.1, bf16[2,16,128,128]{3,2,1,0:T(8,128)(2,1)} %tw_hbm.1, ...), custom_call_target="tpu_custom_call" | custom-call | tf_op jit(solution)/shard_map/sage_layer/pallas_call | solution.py:410
  78.6 1.4 %write_out.1 = (bf16[64,256]{1,0:T(8,128)(2,1)}, f32[4,1024]{1,0:T(4,128)}, f32[4,1024]{1,0:T(4,128)}) custom-call(bf16[64,256]{1,0:T(8,128)(2,1)} %get-tuple-element.8.hidden, f32[8,1024]{1,0:T(8,128)} %get-tuple-element.9.grads), custom_call_target="tpu_custom_call" | custom-call | tf_op jit(solution)/shard_map/write_out/pallas_call | solution.py:472

commit v4 on v3

--- a/solution.py
+++ b/solution.py
@@ -11,12 +11,13 @@
 
 NZ, NY, NX, NC = 16, 8, 4, 2
 NN = NY * NX * NC
-NBAR = NN - 1 + 6
+NBAR = NN - 1 + 8
 
 PARENT = {
     8: 6, -8: -6, 7: 6, 5: 6, -7: -6, -5: -6, 6: 3, -6: -3,
     4: 3, 2: 3, -4: -3, -2: -3, 3: 0, -3: 0, 1: 0, -1: 0,
 }
+UP = {**PARENT, 6: 0, -6: 0}
 LEAVES = (8, -8, 7, -7, 5, -5, 4, -4, 2, -2, 1, -1)
 HALVES = {8: 0, -8: 64}
 GROUPS = ((0, 1, -1, 3), (-3, 2, -2, 4), (-4, 6, -6, 5), (7, -5, -7, 8))
@@ -49,7 +50,7 @@
 def kernel(
     feat, rows_hbm, counts_hbm, seed_hbm, tsrc_hbm, tw_hbm, ws_hbm, wn_hbm, cot_hbm,
     hid, grads,
-    rows, counts, seed, tsrc, slots, src, out, tw, ws, wn, cot, sf, nm, part, pk, pkb, rb, sb, cp, ag, xpt, stack,
+    rows, counts, seed, tsrc, slots, wc, mean, src, out, tw, ws, wn, cot, sf, nm, part, pk, pkb, rb, sb, cp, ag, xpt, stack,
     cs, cr, xs, xb, xr, ys, yb, yr, fin,
     lsem, a_send, a_recv, b_send, b_recv, c_send, c_recv,
     dc_send, dc_recv, dx_send, dx_recv, dy_send, dy_recv,
@@ -79,7 +80,7 @@
             if d or j:
                 to = ((y + d) % NY) * 8 + (node + j) % 8
                 pl.semaphore_signal(barrier, inc=1, device_id=(z, to), device_id_type=MESH)
-    for d in (3, -3, 2, -2, 1, -1):
+    for d in (6, -6, 3, -3, 2, -2, 1, -1):
         pl.semaphore_signal(barrier, inc=1, device_id=(zat(d), node), device_id_type=MESH)
     for load in loads[3:]:
         load.start()
@@ -155,26 +156,40 @@
     for load in loads[6:]:
         load.wait()
 
+    def by_source(t, carry):
+        cols = pl.ds(pl.multiple_of((t % 2) * 128, 128), 128)
+        for b in range(2):
+            total = jnp.zeros((128, 128), F32)
+            for k in range(16):
+                total += jnp.where(tsrc[b, k] == t, tw[b, k].astype(F32), 0.0)
+            high = total.astype(BF16)
+            wc[t // 2, pl.ds(b * 128, 128), cols] = high
+            wc[t // 2, pl.ds(256 + b * 128, 128), cols] = (total - high.astype(F32)).astype(BF16)
+        return carry
+
+    lax.fori_loop(0, 16, by_source, 0)
+
+    def blocks_times(pairs):
+        total = jnp.zeros((512, 256), F32)
+        for pair_of in pairs:
+            block = src[pl.ds(pair_of * 16, 16)].reshape(256, 256)
+            total += jnp.dot(wc[pair_of], block, preferred_element_type=F32)
+        return total[0:256] + total[256:512]
+
+    mean[...] = blocks_times(range(4))
+
     own.wait()
     pltpu.make_async_remote_copy(
         src_ref=src.at[pl.ds(0, NN - 1)], dst_ref=src.at[pl.ds(NN, NN - 1)],
         send_sem=a_send, recv_sem=a_recv, device_id=(z, node), device_id_type=MESH,
     ).wait_recv()
-    for b in range(2):
-        total = jnp.zeros((128, 256), F32)
-        for k in range(0, 16, 2):
-            weight = jnp.concatenate([tw[b, k], tw[b, k + 1]], axis=1)
-            block = jnp.concatenate(
-                [src[pl.ds(tsrc[b, k + e] * 8, 8)].reshape(128, 256) for e in range(2)], axis=0
-            )
-            total += jnp.dot(weight, block, preferred_element_type=F32)
-        nm[pl.ds(b * 128, 128), :] = total.astype(BF16)
+    nm[...] = (mean[...] + blocks_times(range(4, 8))).astype(BF16)
 
     def up(o, source):
         return pltpu.make_async_remote_copy(
             src_ref=rows_of(source, o), dst_ref=rows_of(rb.at[slot(o)], o),
             send_sem=b_send.at[sem(o)], recv_sem=b_recv.at[sem(o)],
-            device_id=(zat(PARENT[o] - o), node), device_id_type=MESH,
+            device_id=(zat(UP[o] - o), node), device_id_type=MESH,
         )
 
     ups = {o: up(o, pkb.at[zat(-o)]) for o in LEAVES}
@@ -226,9 +241,9 @@
     hand_up(-6, (-7, -8, -5))
     ups[1].start()
     ups[-1].start()
-    hand_up(3, (4, 2, 6))
-    hand_up(-3, (-4, -2, -6))
-    pre = summed(0, (1, -1, 3, -3))
+    hand_up(3, (4, 2))
+    hand_up(-3, (-4, -2))
+    pre = summed(0, (1, -1, 3, -3, 6, -6))
 
     s = jax.nn.sigmoid(pre)
     slope = s * (1.0 + pre * (1.0 - s))
@@ -421,6 +436,8 @@
             pltpu.VMEM((2, 128), jnp.int32),
             pltpu.SMEM((2, 16), jnp.int32),
             pltpu.VMEM((128, 128), F32),
+            pltpu.VMEM((8, 512, 256), BF16),
+            pltpu.VMEM((256, 256), F32),
             pltpu.VMEM((2 * NN, 16, 256), BF16),
             pltpu.VMEM((NN, 16, 256), BF16),
             pltpu.VMEM((2, 16, 128, 128), BF16),

time: 80.2 us -> 80.6 us (level)
  no operation moved by 1% of the time
where the time goes in v4:
time: 80.6 us; the launch traced here: 80.4 us
  Pallas kernels  79.7 us (99%)
    pallas_call x1, Pallas kernels, on_device(): pl.pallas_call(kernel, out_shape=(jax.ShapeDtypeStruct((64, 256), BF16),...  78.3 us

profile of v4, /device:TPU:1, one launch (start us, length us, event | category | flops | bytes accessed | tf_op | source)
XLA Modules:
  0.0 80.4 jit_solution(6475371540253746628)
XLA Ops:
  0.6 78.3 %sage_layer.1 = (bf16[64,256]{1,0:T(8,128)(2,1)}, f32[8,1024]{1,0:T(8,128)}) custom-call(bf16[64,16,256]{2,1,0:T(8,128)(2,1)} %bitcast.6, s32[16,64]{1,0:T(8,128)} %bitcast.7, s32[1,64]{1,0:T(1,128)} %counts_hbm.1, s32[2,128]{1,0:T(2,128)} %bitcast.8, s32[2,16]{1,0:T(2,128)} %tsrc_hbm.1, bf16[2,16,128,128]{3,2,1,0:T(8,128)(2,1)} %tw_hbm.1, ...), custom_call_target="tpu_custom_call" | custom-call | tf_op jit(solution)/shard_map/sage_layer/pallas_call | solution.py:425
  79.0 1.4 %write_out.1 = (bf16[64,256]{1,0:T(8,128)(2,1)}, f32[4,1024]{1,0:T(4,128)}, f32[4,1024]{1,0:T(4,128)}) custom-call(bf16[64,256]{1,0:T(8,128)(2,1)} %get-tuple-element.8.hidden, f32[8,1024]{1,0:T(8,128)} %get-tuple-element.9.grads), custom_call_target="tpu_custom_call" | custom-call | tf_op jit(solution)/shard_map/write_out/pallas_call | solution.py:489
